TPU v7x, 256 devices: a whole 4x4x8 slice. The times are simulated.
256 devices in a mesh: dp: 8 (over z_lo, core), seq: 32 (over y, x, z_hi).
Axes of the slice: x: 4, y: 4, z: 8 (z_hi: 2, z_lo: 4; z = z_hi * 4 + z_lo), core: 2. Of those that a mesh axis runs over, the one named last changes fastest.
Arguments:
- first_input: bfloat16 [8, 16384, 128], P('dp', 'seq'), may hold values from -6 to 6
- value_input: bfloat16 [8, 16384, 128], P('dp', 'seq'), may hold values from -6 to 6
- gate_input: bfloat16 [8, 16384, 128], P('dp', 'seq'), may hold values from -6 to 6
- cotangent: bfloat16 [8, 16384, 128], P('dp', 'seq'), may hold values from -6 to 6
- filter_taps: float32 [16384, 128], P('seq'), may hold values from -4 to 4
- skip_weight: float32 [128], replicated, may hold values from -4 to 4
Outputs:
- layer_output: bfloat16 [8, 16384, 128], P('dp', 'seq')
- filter_grad: float32 [16384, 128], P('seq')
All inputs are finite; a program needn't handle non-finite values.
Results may differ from a plain program's by a relative error of at most 0.001.
Values sent between devices are 32-bit elements; how exact they have to be, the bound alone decides.
A program may use at most 64 MiB of HBM per device.

v0:
```python
import functools
import math
import jax
import jax.numpy as jnp
from jax import lax
from jax.sharding import PartitionSpec as P


def angles(numer, period):
    return 2.0 * math.pi / period * (numer % period).astype(jnp.float32)


def rotate(real_part, imag_part, phase, direction):
    cosine = jnp.cos(phase)
    sine = direction * jnp.sin(phase)
    return (real_part * cosine - imag_part * sine, real_part * sine + imag_part * cosine)


def local_transform(real_part, imag_part, direction):
    count, length = real_part.shape
    outer = 1 << (length.bit_length() - 1) // 2
    inner = length // outer
    real_cube = real_part.reshape(count, outer, inner)
    imag_cube = imag_part.reshape(count, outer, inner)
    outer_idx = lax.iota(jnp.int32, outer)
    inner_idx = lax.iota(jnp.int32, inner)
    first_phase = angles(outer_idx[:, None] * outer_idx[None, :], outer)
    first_cos = jnp.cos(first_phase)
    first_sin = direction * jnp.sin(first_phase)
    mix = functools.partial(
        jnp.einsum, precision=lax.Precision.HIGHEST, preferred_element_type=jnp.float32
    )
    section_real = mix("kp,cpq->ckq", first_cos, real_cube) - mix(
        "kp,cpq->ckq", first_sin, imag_cube
    )
    section_imag = mix("kp,cpq->ckq", first_cos, imag_cube) + mix(
        "kp,cpq->ckq", first_sin, real_cube
    )
    twiddle = angles(outer_idx[:, None] * inner_idx[None, :], length)
    section_real, section_imag = rotate(section_real, section_imag, twiddle, direction)
    second_phase = angles(inner_idx[:, None] * inner_idx[None, :], inner)
    second_cos = jnp.cos(second_phase)
    second_sin = direction * jnp.sin(second_phase)
    final_real = mix("ckq,jq->ckj", section_real, second_cos) - mix(
        "ckq,jq->ckj", section_imag, second_sin
    )
    final_imag = mix("ckq,jq->ckj", section_imag, second_cos) + mix(
        "ckq,jq->ckj", section_real, second_sin
    )
    final_real = jnp.transpose(final_real, (0, 2, 1)).reshape(count, length)
    final_imag = jnp.transpose(final_imag, (0, 2, 1)).reshape(count, length)
    return (final_real, final_imag)


def channel_layout(gated, weighted, filter_taps, gate_input, skip_weight):
    batch_local = gated.shape[0]
    moved_gated, moved_weighted, moved_taps = (
        lax.all_to_all(gated, "seq", split_axis=2, concat_axis=1, tiled=True),
        lax.all_to_all(weighted, "seq", split_axis=2, concat_axis=1, tiled=True),
        lax.all_to_all(filter_taps[None], "seq", split_axis=2, concat_axis=1, tiled=True),
    )
    length = moved_gated.shape[1]
    narrow = moved_gated.shape[2]
    spread = batch_local * narrow
    gated_rows = jnp.transpose(moved_gated, (0, 2, 1)).reshape(spread, length)
    weighted_rows = jnp.transpose(moved_weighted, (0, 2, 1)).reshape(spread, length)
    taps_rows = jnp.transpose(moved_taps[0], (1, 0))
    rows_all = jnp.concatenate([gated_rows, taps_rows, weighted_rows], axis=0)
    count = rows_all.shape[0]
    twist = angles(lax.iota(jnp.int32, length), 2 * length)[None, :]
    cos_twist = jnp.cos(twist)
    sin_twist = jnp.sin(twist)
    real_in = jnp.concatenate([rows_all, rows_all * cos_twist], axis=0)
    imag_in = jnp.concatenate([jnp.zeros_like(rows_all), -rows_all * sin_twist], axis=0)
    spec_real, spec_imag = local_transform(real_in, imag_in, -1.0)
    spec_real = spec_real.reshape(2, count, length)
    spec_imag = spec_imag.reshape(2, count, length)
    gated_real = spec_real[:, :spread].reshape(2, batch_local, narrow, length)
    gated_imag = spec_imag[:, :spread].reshape(2, batch_local, narrow, length)
    taps_real = spec_real[:, spread : spread + narrow][:, None]
    taps_imag = spec_imag[:, spread : spread + narrow][:, None]
    source_real = spec_real[:, spread + narrow :].reshape(2, batch_local, narrow, length)
    source_imag = spec_imag[:, spread + narrow :].reshape(2, batch_local, narrow, length)
    conv_real = (gated_real * taps_real - gated_imag * taps_imag).reshape(2, spread, length)
    conv_imag = (gated_real * taps_imag + gated_imag * taps_real).reshape(2, spread, length)
    grad_real = jnp.sum(source_real * gated_real + source_imag * gated_imag, axis=1)
    grad_imag = jnp.sum(source_imag * gated_real - source_real * gated_imag, axis=1)
    back_real = jnp.concatenate([conv_real, grad_real], axis=1).reshape(-1, length)
    back_imag = jnp.concatenate([conv_imag, grad_imag], axis=1).reshape(-1, length)
    back_real, back_imag = local_transform(back_real, back_imag, 1.0)
    back_real = back_real.reshape(2, -1, length)
    back_imag = back_imag.reshape(2, -1, length)
    joined = (back_real[0] + back_real[1] * cos_twist - back_imag[1] * sin_twist) / (2.0 * length)
    convolved = jnp.transpose(joined[:spread].reshape(batch_local, narrow, length), (0, 2, 1))
    grad_time = lax.psum(jnp.transpose(joined[spread:], (1, 0)), "dp")
    convolved, grad_back = (
        lax.all_to_all(convolved, "seq", split_axis=1, concat_axis=2, tiled=True),
        lax.all_to_all(grad_time[None], "seq", split_axis=1, concat_axis=2, tiled=True),
    )
    layer_output = (gate_input.astype(jnp.float32) * (convolved + skip_weight * gated)).astype(
        jnp.bfloat16
    )
    scale = 1.0 / math.sqrt(batch_local * lax.axis_size("dp") * length)
    return (layer_output, grad_back[0] * scale)


def shards(first_input, value_input, gate_input, cotangent, filter_taps, skip_weight):
    gated = first_input.astype(jnp.float32) * value_input.astype(jnp.float32)
    weighted = cotangent.astype(jnp.float32) * gate_input.astype(jnp.float32)
    return channel_layout(gated, weighted, filter_taps, gate_input, skip_weight)


def solution(mesh):
    placed = (
        P("dp", "seq", None),
        P("dp", "seq", None),
        P("dp", "seq", None),
        P("dp", "seq", None),
        P("seq", None),
        P(),
    )
    return jax.shard_map(
        shards,
        mesh=mesh,
        in_specs=placed,
        out_specs=(P("dp", "seq", None), P("seq", None)),
        check_vma=False,
    )
```

profile of v0, /device:TPU:2, one launch (start us, length us, event | category | flops | bytes accessed | tf_op | source)
XLA Modules:
  0.0 486.5 jit_solution(10669566144408117033)
XLA Ops:
  9.1 14.2 %all-to-all-start.2 = ((f32[1,512,128]{1,0,2:T(1,128)}), f32[1,512,128]{1,0,2:T(1,128)S(1)}, u32[]{:S(2)}, u32[]{:S(2)}) async-start(f32[1,512,128]{1,0,2:T(1,128)} %copy.157), calls=%async_computation.2 | async-start | bytes 524288 | tf_op jit(solution)/shard_map/all_to_all | solution.py:59
  24.2 11.4 %all-to-all-done.2 = f32[1,512,128]{1,0,2:T(1,128)S(1)} async-done(((f32[1,512,128]{1,0,2:T(1,128)}), f32[1,512,128]{1,0,2:T(1,128)S(1)}, u32[]{:S(2)}, u32[]{:S(2)}) %all-to-all-start.2) | async-done | bytes 262176 | tf_op jit(solution)/shard_map/all_to_all | solution.py:59
  35.6 5.0 %all-to-all-start.1 = ((f32[1,512,128]{1,0,2:T(1,128)}), f32[1,512,128]{1,0,2:T(1,128)S(1)}, u32[]{:S(2)}, u32[]{:S(2)}) async-start(f32[1,512,128]{1,0,2:T(1,128)} %copy.211), calls=%async_computation.1 | async-start | bytes 524288 | tf_op jit(solution)/shard_map/all_to_all | solution.py:60
  42.2 10.6 %all-to-all-done.1 = f32[1,512,128]{1,0,2:T(1,128)S(1)} async-done(((f32[1,512,128]{1,0,2:T(1,128)}), f32[1,512,128]{1,0,2:T(1,128)S(1)}, u32[]{:S(2)}, u32[]{:S(2)}) %all-to-all-start.1) | async-done | bytes 262176 | tf_op jit(solution)/shard_map/all_to_all | solution.py:60
  52.9 6.1 %all-to-all-start = ((f32[1,512,128]{1,0,2:T(1,128)}), f32[1,512,128]{1,0,2:T(1,128)S(1)}, u32[]{:S(2)}, u32[]{:S(2)}) async-start(f32[1,512,128]{1,0,2:T(1,128)} %copy.153), calls=%async_computation | async-start | bytes 524288 | tf_op jit(solution)/shard_map/all_to_all | solution.py:58
  62.3 8.7 %all-to-all-done = f32[1,512,128]{1,0,2:T(1,128)S(1)} async-done(((f32[1,512,128]{1,0,2:T(1,128)}), f32[1,512,128]{1,0,2:T(1,128)S(1)}, u32[]{:S(2)}, u32[]{:S(2)}) %all-to-all-start) | async-done | bytes 262176 | tf_op jit(solution)/shard_map/all_to_all | solution.py:58
  81.1 3.4 fusion.11
  84.5 4.0 fusion.15
  88.5 4.0 add_bitcast_fusion
  98.6 5.4 %subtract_bitcast_fusion = f32[24,128,128]{1,2,0:T(8,128)} fusion(f32[24,128,128]{2,1,0:T(8,128)} %fusion.15, f32[24,128,128]{2,1,0:T(8,128)S(1)} %convolution_add_fusion, f32[24,128,128]{2,1,0:T(8,128)S(1)} %convolution_subtract_fusion, f32[128,128]{0,1:T(8,128)S(1)} %copy.169, f32[128,128]{0,1:T(8,128)S(1)} %copy.167), kind=kOutput, calls=%fused_computation.8 | convolution fusion | flops 605798400 | bytes 6422528 | tf_op jit(solution)/shard_map/ckq,jq->ckj/dot_general | solution.py:44
  104.0 3.2 copy.172
  135.5 12.0 %copy.189 = f32[1,16384,4]{2,0,1:T(1,128)} copy(f32[1,16384,4]{1,2,0:T(4,128)S(1)} %get-tuple-element.17) | data formatting | bytes 524288 | tf_op jit(solution)/shard_map/transpose | solution.py:94
  148.0 74.5 %reduce = f32[16384,4]{1,0:T(8,128)} reduce(f32[16384,1,4]{2,1,0:T(1,128)} %bitcast.179, f32[]{:T(128)} %broadcast.236), dimensions={1}, to_apply=%bitcast.163.reduce_sub_computation | reduce | bytes 524292
  222.6 9.5 %reshape.143 = f32[32,1,2048]{2,1,0:T(1,128)} reshape(f32[16384,4]{1,0:T(8,128)} %reduce) | data formatting | bytes 524288
  232.0 5.9 %all-to-all-start.3 = ((f32[32,1,2048]{2,1,0:T(1,128)}), f32[32,1,2048]{2,1,0:T(1,128)S(1)}, u32[]{:S(2)}, u32[]{:S(2)}) async-start(f32[32,1,2048]{2,1,0:T(1,128)} %reshape.143), calls=%async_computation.3 | async-start | bytes 524288 | tf_op jit(solution)/shard_map/all_to_all | solution.py:97
  238.7 77.0 %all-reduce.3.cloned.1.call-done = f32[1,16384,4]{1,2,0:T(4,128)} async-done(((f32[1,16384,4]{1,2,0:T(4,128)}), f32[1,16384,4]{1,2,0:T(4,128)}) %all-reduce.3.cloned.1.call-update) | async-done | bytes 262160 | tf_op jit(solution)/shard_map/psum | solution.py:95
  315.7 14.8 %copy.193 = f32[1,16384,4]{2,0,1:T(1,128)} copy(f32[1,16384,4]{1,2,0:T(4,128)} %all-reduce.3.cloned.1.call-done) | data formatting | bytes 524288 | tf_op jit(solution)/shard_map/psum | solution.py:95
  330.6 74.5 %reduce.2 = f32[16384,4]{1,0:T(8,128)} reduce(f32[16384,1,4]{2,1,0:T(1,128)} %bitcast.180, f32[]{:T(128)} %broadcast.236), dimensions={1}, to_apply=%bitcast.165.reduce_sub_computation | reduce | bytes 524292
  405.1 9.1 %reshape.145 = f32[32,1,2048]{2,1,0:T(1,128)} reshape(f32[16384,4]{1,0:T(8,128)} %reduce.2) | data formatting | bytes 524288
  414.2 10.4 %all-to-all-start.4 = ((f32[32,1,2048]{2,1,0:T(1,128)}), f32[32,1,2048]{2,1,0:T(1,128)S(1)}, u32[]{:S(2)}, u32[]{:S(2)}) async-start(f32[32,1,2048]{2,1,0:T(1,128)} %reshape.145), calls=%async_computation.4 | async-start | bytes 524288 | tf_op jit(solution)/shard_map/all_to_all | solution.py:98
  425.9 14.8 %reshape.144 = f32[16384,1,4]{2,1,0:T(1,128)} reshape(f32[32,2048]{1,0:T(8,128)S(1)} %reduce.1) | data formatting | bytes 524288
  440.6 5.3 %copy.212 = f32[1,32,512,4]{2,1,3,0:T(8,128)S(1)} copy(f32[1,32,512,4]{3,2,1,0:T(8,128)} %bitcast.181) | data formatting | bytes 524288 | tf_op jit(solution)/shard_map/all_to_all | solution.py:97
  448.4 14.8 %reshape.146 = f32[16384,1,4]{2,1,0:T(1,128)} reshape(f32[32,2048]{1,0:T(8,128)S(1)} %reduce.3) | data formatting | bytes 524288
  463.2 15.0 %copy.194 = f32[1,16384,4]{1,2,0:T(4,128)S(1)} copy(f32[1,16384,4]{2,0,1:T(1,128)} %bitcast.182) | data formatting | bytes 524288 | tf_op jit(solution)/shard_map/all_to_all | solution.py:98
  (106 shorter events, 58.0 us)
Async XLA Ops:
  7.2 16.2 %copy-start.15 = (f32[512,128]{1,0:T(8,128)S(1)}, f32[512,128]{1,0:T(8,128)}, u32[]{:S(2)}) copy-start(f32[512,128]{1,0:T(8,128)} %param.10) | copy-start | bytes 786436
  7.2 33.4 %copy-start.10 = (bf16[1,512,128]{2,1,0:T(8,128)(2,1)S(1)}, bf16[1,512,128]{2,1,0:T(8,128)(2,1)}, u32[]{:S(2)}) copy-start(bf16[1,512,128]{2,1,0:T(8,128)(2,1)} %param.7) | copy-start | bytes 393220
  7.2 33.4 %copy-start.12 = (bf16[1,512,128]{2,1,0:T(8,128)(2,1)S(1)}, bf16[1,512,128]{2,1,0:T(8,128)(2,1)}, u32[]{:S(2)}) copy-start(bf16[1,512,128]{2,1,0:T(8,128)(2,1)} %param.6) | copy-start | bytes 393220
  9.1 26.5 %all-to-all-start.2 = ((f32[1,512,128]{1,0,2:T(1,128)}), f32[1,512,128]{1,0,2:T(1,128)S(1)}, u32[]{:S(2)}, u32[]{:S(2)}) async-start(f32[1,512,128]{1,0,2:T(1,128)} %copy.157), calls=%async_computation.2 | async-start | bytes 524288 | tf_op jit(solution)/shard_map/all_to_all | solution.py:59
  35.6 17.3 %all-to-all-start.1 = ((f32[1,512,128]{1,0,2:T(1,128)}), f32[1,512,128]{1,0,2:T(1,128)S(1)}, u32[]{:S(2)}, u32[]{:S(2)}) async-start(f32[1,512,128]{1,0,2:T(1,128)} %copy.211), calls=%async_computation.1 | async-start | bytes 524288 | tf_op jit(solution)/shard_map/all_to_all | solution.py:60
  52.9 18.1 %all-to-all-start = ((f32[1,512,128]{1,0,2:T(1,128)}), f32[1,512,128]{1,0,2:T(1,128)S(1)}, u32[]{:S(2)}, u32[]{:S(2)}) async-start(f32[1,512,128]{1,0,2:T(1,128)} %copy.153), calls=%async_computation | async-start | bytes 524288 | tf_op jit(solution)/shard_map/all_to_all | solution.py:58
  60.5 10.9 %copy-start.7 = (f32[16384]{0:T(1024)}, f32[16384]{0:T(1024)S(1)}, u32[]{:S(2)}) copy-start(f32[16384]{0:T(1024)S(1)} %fusion.51) | copy-start | bytes 196612
  62.3 9.8 %copy-start.1 = (f32[4,128,128]{1,2,0:T(8,128)}, f32[4,128,128]{1,2,0:T(8,128)S(1)}, u32[]{:S(2)}) copy-start(f32[4,128,128]{1,2,0:T(8,128)S(1)} %copy.164) | copy-start | bytes 786436
  71.4 0.7 copy-start.3
  76.6 2.9 copy-start.2
  76.6 2.9 copy-start.4
  107.2 3.2 copy-start
  119.5 1.9 copy-start.6
  132.7 1.0 copy-start.5
  132.7 1.0 copy-start.8
  132.7 1.0 copy-start.14
  232.0 182.2 %all-to-all-start.3 = ((f32[32,1,2048]{2,1,0:T(1,128)}), f32[32,1,2048]{2,1,0:T(1,128)S(1)}, u32[]{:S(2)}, u32[]{:S(2)}) async-start(f32[32,1,2048]{2,1,0:T(1,128)} %reshape.143), calls=%async_computation.3 | async-start | bytes 524288 | tf_op jit(solution)/shard_map/all_to_all | solution.py:97
  238.0 77.8 %all-reduce.3.cloned.1.call-start = ((), (), s32[]{:S(2)}) async-start(), calls=%async_computation.5 | async-start | bytes 524288 | tf_op jit(solution)/shard_map/psum | solution.py:95
  414.2 33.0 %all-to-all-start.4 = ((f32[32,1,2048]{2,1,0:T(1,128)}), f32[32,1,2048]{2,1,0:T(1,128)S(1)}, u32[]{:S(2)}, u32[]{:S(2)}) async-start(f32[32,1,2048]{2,1,0:T(1,128)} %reshape.145), calls=%async_computation.4 | async-start | bytes 524288 | tf_op jit(solution)/shard_map/all_to_all | solution.py:98
  440.6 5.7 %copy-start.9 = (bf16[1,512,128]{2,1,0:T(8,128)(2,1)S(1)}, bf16[1,512,128]{2,1,0:T(8,128)(2,1)}, u32[]{:S(2)}) copy-start(bf16[1,512,128]{2,1,0:T(8,128)(2,1)} %param.8) | copy-start | bytes 393220
  440.6 5.7 %copy-start.11 = (bf16[1,512,128]{2,1,0:T(8,128)(2,1)S(1)}, bf16[1,512,128]{2,1,0:T(8,128)(2,1)}, u32[]{:S(2)}) copy-start(bf16[1,512,128]{2,1,0:T(8,128)(2,1)} %param.7) | copy-start | bytes 393220
  440.6 5.7 %copy-start.13 = (bf16[1,512,128]{2,1,0:T(8,128)(2,1)S(1)}, bf16[1,512,128]{2,1,0:T(8,128)(2,1)}, u32[]{:S(2)}) copy-start(bf16[1,512,128]{2,1,0:T(8,128)(2,1)} %param.6) | copy-start | bytes 393220
  440.6 5.7 %copy-start.16 = (f32[128]{0:T(128)S(1)}, f32[128]{0:T(128)}, u32[]{:S(2)}) copy-start(f32[128]{0:T(128)} %param.11) | copy-start | bytes 1540
Sparse Core Ops, SparseCore 0:
  242.0 73.7 all-reduce.2
where the time goes:
time: 491 us; the launch traced here: 486 us
  other arithmetic  160 us (33%)
  local copies, waits for them, and re-layouts  120 us (24%)
  waiting for transfers between devices  108 us (22%)
  starting transfers between devices  41.7 us (8%)
  matrix products  41.6 us (8%)
  between operations  14.9 us (3%)
    unnamed x3, other arithmetic  149 us
    psum x1, waiting for transfers between devices, channel_layout(): grad_time = lax.psum(jnp.transpose(joined[spread:], (1, 0)), 'dp')  77 us
    unnamed x49, local copies, waits for them, and re-layouts  51.3 us
    all_to_all x1, local copies, waits for them, and re-layouts, channel_layout(): lax.all_to_all(grad_time[None], 'seq', split_axis=1, concat_axis=2, tiled...  15 us
    psum x1, local copies, waits for them, and re-layouts, channel_layout(): grad_time = lax.psum(jnp.transpose(joined[spread:], (1, 0)), 'dp')  14.8 us
    all_to_all x1, starting transfers between devices, channel_layout(): lax.all_to_all(weighted, 'seq', split_axis=2, concat_axis=1, tiled=True)  14.2 us
    transpose x1, local copies, waits for them, and re-layouts, channel_layout(): jnp.transpose(joined[:spread].reshape(batch_local, narrow, length), (0, 2...  12 us
    all_to_all x1, waiting for transfers between devices, channel_layout(): lax.all_to_all(weighted, 'seq', split_axis=2, concat_axis=1, tiled=True)  11.4 us
  transfers between devices with their start and end apart: 6, of which 4 were waited for; matrix products, arithmetic and copies ran while one was open for 26% of the time, Pallas kernels for 0%

commit v1 on v0

--- a/solution.py
+++ b/solution.py
@@ -4,6 +4,12 @@
 import jax.numpy as jnp
 from jax import lax
 from jax.sharding import PartitionSpec as P
+
+
+def trade_parts(block, axis, split, join):
+    pieces = jnp.split(block, lax.axis_size(axis), axis=split)
+    incoming = lax.all_to_all(jnp.stack(pieces), axis, 0, 0)
+    return jnp.concatenate(incoming, axis=join)
 
 
 def angles(numer, period):
@@ -55,7 +61,7 @@
 def channel_layout(gated, weighted, filter_taps, gate_input, skip_weight):
     batch_local = gated.shape[0]
     moved_gated, moved_weighted, moved_taps = (
-        lax.all_to_all(gated, "seq", split_axis=2, concat_axis=1, tiled=True),
+        trade_parts(gated, "seq", 2, 1),
         lax.all_to_all(weighted, "seq", split_axis=2, concat_axis=1, tiled=True),
         lax.all_to_all(filter_taps[None], "seq", split_axis=2, concat_axis=1, tiled=True),
     )

time: 491 us -> 495 us (level)
    all_to_all x1, starting transfers between devices: 14.2 us -> 4.98 us  [channel_layout(): lax.all_to_all(weighted, 'seq', split_axis=2, concat_axis=1, tiled=True)]
    all_to_all x1, starting transfers between devices: 6.13 us -> 14.2 us  [trade_parts(): incoming = lax.all_to_all(jnp.stack(pieces), axis, 0, 0)]
    unnamed x49 -> x56, local copies, waits for them, and re-layouts: 51.3 us -> 55.1 us
where the time goes in v1:
time: 495 us; the launch traced here: 489 us
  other arithmetic  160 us (32%)
  local copies, waits for them, and re-layouts  123 us (25%)
  waiting for transfers between devices  108 us (22%)
  starting transfers between devices  42 us (8%)
  matrix products  41.4 us (8%)
  between operations  14.9 us (3%)
    unnamed x3, other arithmetic  149 us
    psum x1, waiting for transfers between devices, channel_layout(): grad_time = lax.psum(jnp.transpose(joined[spread:], (1, 0)), 'dp')  77 us
    unnamed x56, local copies, waits for them, and re-layouts  55.1 us
    all_to_all x1, local copies, waits for them, and re-layouts, channel_layout(): lax.all_to_all(grad_time[None], 'seq', split_axis=1, concat_axis=2, tiled...  15 us
    psum x1, local copies, waits for them, and re-layouts, channel_layout(): grad_time = lax.psum(jnp.transpose(joined[spread:], (1, 0)), 'dp')  14.8 us
    all_to_all x1, starting transfers between devices, trade_parts(): incoming = lax.all_to_all(jnp.stack(pieces), axis, 0, 0)  14.2 us
    transpose x1, local copies, waits for them, and re-layouts, channel_layout(): jnp.transpose(joined[:spread].reshape(batch_local, narrow, length), (0, 2...  12 us
    all_to_all x1, waiting for transfers between devices, channel_layout(): lax.all_to_all(weighted, 'seq', split_axis=2, concat_axis=1, tiled=True)  10.7 us
  transfers between devices with their start and end apart: 6, of which 4 were waited for; matrix products, arithmetic and copies ran while one was open for 26% of the time, Pallas kernels for 0%

profile of v1, /device:TPU:2, one launch (start us, length us, event | category | flops | bytes accessed | tf_op | source)
XLA Modules:
  0.0 489.1 jit_solution(3527387899514724409)
XLA Ops:
  11.9 14.2 %all-to-all-start = ((f32[32,1,512,4]{2,3,1,0:T(4,128)}), f32[32,1,512,4]{2,3,1,0:T(4,128)S(1)}, u32[]{:S(2)}, u32[]{:S(2)}) async-start(f32[32,1,512,4]{2,3,1,0:T(4,128)} %copy.153), calls=%async_computation | async-start | bytes 524288 | tf_op jit(solution)/shard_map/all_to_all | solution.py:11
  27.7 10.7 %all-to-all-done = f32[32,1,512,4]{2,3,1,0:T(4,128)S(1)} async-done(((f32[32,1,512,4]{2,3,1,0:T(4,128)}), f32[32,1,512,4]{2,3,1,0:T(4,128)S(1)}, u32[]{:S(2)}, u32[]{:S(2)}) %all-to-all-start) | async-done | bytes 262176 | tf_op jit(solution)/shard_map/all_to_all | solution.py:11
  38.3 5.0 %all-to-all-start.2 = ((f32[1,512,128]{1,0,2:T(1,128)}), f32[1,512,128]{1,0,2:T(1,128)S(1)}, u32[]{:S(2)}, u32[]{:S(2)}) async-start(f32[1,512,128]{1,0,2:T(1,128)} %convert_multiply_fusion), calls=%async_computation.2 | async-start | bytes 524288 | tf_op jit(solution)/shard_map/all_to_all | solution.py:65
  44.9 10.7 %all-to-all-done.2 = f32[1,512,128]{1,0,2:T(1,128)S(1)} async-done(((f32[1,512,128]{1,0,2:T(1,128)}), f32[1,512,128]{1,0,2:T(1,128)S(1)}, u32[]{:S(2)}, u32[]{:S(2)}) %all-to-all-start.2) | async-done | bytes 262176 | tf_op jit(solution)/shard_map/all_to_all | solution.py:65
  55.6 6.3 %all-to-all-start.1 = ((f32[1,512,128]{1,0,2:T(1,128)}), f32[1,512,128]{1,0,2:T(1,128)S(1)}, u32[]{:S(2)}, u32[]{:S(2)}) async-start(f32[1,512,128]{1,0,2:T(1,128)} %copy.211), calls=%async_computation.1 | async-start | bytes 524288 | tf_op jit(solution)/shard_map/all_to_all | solution.py:66
  65.0 8.7 %all-to-all-done.1 = f32[1,512,128]{1,0,2:T(1,128)S(1)} async-done(((f32[1,512,128]{1,0,2:T(1,128)}), f32[1,512,128]{1,0,2:T(1,128)S(1)}, u32[]{:S(2)}, u32[]{:S(2)}) %all-to-all-start.1) | async-done | bytes 262176 | tf_op jit(solution)/shard_map/all_to_all | solution.py:66
  86.9 4.0 fusion.15
  90.9 4.0 add_bitcast_fusion
  101.0 5.4 %subtract_bitcast_fusion = f32[24,128,128]{1,2,0:T(8,128)} fusion(f32[24,128,128]{2,1,0:T(8,128)} %fusion.15, f32[24,128,128]{2,1,0:T(8,128)S(1)} %convolution_add_fusion, f32[24,128,128]{2,1,0:T(8,128)S(1)} %convolution_subtract_fusion, f32[128,128]{0,1:T(8,128)S(1)} %copy.169, f32[128,128]{0,1:T(8,128)S(1)} %copy.167), kind=kOutput, calls=%fused_computation.8 | convolution fusion | flops 605798400 | bytes 6422528 | tf_op jit(solution)/shard_map/ckq,jq->ckj/dot_general | solution.py:50
  106.4 3.3 copy.172
  109.6 3.2 reshape_reshape.14
  138.1 12.0 %copy.189 = f32[1,16384,4]{2,0,1:T(1,128)} copy(f32[1,16384,4]{1,2,0:T(4,128)S(1)} %get-tuple-element.17) | data formatting | bytes 524288 | tf_op jit(solution)/shard_map/transpose | solution.py:100
  150.7 74.4 %reduce = f32[16384,4]{1,0:T(8,128)} reduce(f32[16384,1,4]{2,1,0:T(1,128)} %bitcast.243, f32[]{:T(128)} %broadcast.236), dimensions={1}, to_apply=%bitcast.227.reduce_sub_computation | reduce | bytes 524292
  225.1 9.2 %reshape.147 = f32[32,1,2048]{2,1,0:T(1,128)} reshape(f32[16384,4]{1,0:T(8,128)} %reduce) | data formatting | bytes 524288
  234.3 6.0 %all-to-all-start.3 = ((f32[32,1,2048]{2,1,0:T(1,128)}), f32[32,1,2048]{2,1,0:T(1,128)S(1)}, u32[]{:S(2)}, u32[]{:S(2)}) async-start(f32[32,1,2048]{2,1,0:T(1,128)} %reshape.147), calls=%async_computation.3 | async-start | bytes 524288 | tf_op jit(solution)/shard_map/all_to_all | solution.py:103
  241.0 77.0 %all-reduce.3.cloned.1.call-done = f32[1,16384,4]{1,2,0:T(4,128)} async-done(((f32[1,16384,4]{1,2,0:T(4,128)}), f32[1,16384,4]{1,2,0:T(4,128)}) %all-reduce.3.cloned.1.call-update) | async-done | bytes 262160 | tf_op jit(solution)/shard_map/psum | solution.py:101
  318.0 14.8 %copy.192 = f32[1,16384,4]{2,0,1:T(1,128)} copy(f32[1,16384,4]{1,2,0:T(4,128)} %all-reduce.3.cloned.1.call-done) | data formatting | bytes 524288 | tf_op jit(solution)/shard_map/psum | solution.py:101
  332.8 74.4 %reduce.2 = f32[16384,4]{1,0:T(8,128)} reduce(f32[16384,1,4]{2,1,0:T(1,128)} %bitcast.244, f32[]{:T(128)} %broadcast.236), dimensions={1}, to_apply=%bitcast.229.reduce_sub_computation | reduce | bytes 524292
  407.3 9.1 %reshape.149 = f32[32,1,2048]{2,1,0:T(1,128)} reshape(f32[16384,4]{1,0:T(8,128)} %reduce.2) | data formatting | bytes 524288
  416.3 10.4 %all-to-all-start.4 = ((f32[32,1,2048]{2,1,0:T(1,128)}), f32[32,1,2048]{2,1,0:T(1,128)S(1)}, u32[]{:S(2)}, u32[]{:S(2)}) async-start(f32[32,1,2048]{2,1,0:T(1,128)} %reshape.149), calls=%async_computation.4 | async-start | bytes 524288 | tf_op jit(solution)/shard_map/all_to_all | solution.py:104
  428.0 14.8 %reshape.148 = f32[16384,1,4]{2,1,0:T(1,128)} reshape(f32[32,2048]{1,0:T(8,128)S(1)} %reduce.1) | data formatting | bytes 524288
  442.8 5.3 %copy.212 = f32[1,32,512,4]{2,1,3,0:T(8,128)S(1)} copy(f32[1,32,512,4]{3,2,1,0:T(8,128)} %bitcast.245) | data formatting | bytes 524288 | tf_op jit(solution)/shard_map/all_to_all | solution.py:103
  451.0 14.8 %reshape.150 = f32[16384,1,4]{2,1,0:T(1,128)} reshape(f32[32,2048]{1,0:T(8,128)S(1)} %reduce.3) | data formatting | bytes 524288
  465.7 15.0 %copy.193 = f32[1,16384,4]{1,2,0:T(4,128)S(1)} copy(f32[1,16384,4]{2,0,1:T(1,128)} %bitcast.246) | data formatting | bytes 524288 | tf_op jit(solution)/shard_map/all_to_all | solution.py:104
  (112 shorter events, 61.5 us)
Async XLA Ops:
  8.3 17.9 %copy-start.15 = (bf16[1,512,128]{2,1,0:T(8,128)(2,1)S(1)}, bf16[1,512,128]{2,1,0:T(8,128)(2,1)}, u32[]{:S(2)}) copy-start(bf16[1,512,128]{2,1,0:T(8,128)(2,1)} %param.8) | copy-start | bytes 393220
  9.4 16.9 %copy-start.16 = (bf16[1,512,128]{2,1,0:T(8,128)(2,1)S(1)}, bf16[1,512,128]{2,1,0:T(8,128)(2,1)}, u32[]{:S(2)}) copy-start(bf16[1,512,128]{2,1,0:T(8,128)(2,1)} %param.9) | copy-start | bytes 393220
  9.8 0.7 copy-start.5
  11.0 32.3 %copy-start.14 = (f32[512,128]{1,0:T(8,128)S(1)}, f32[512,128]{1,0:T(8,128)}, u32[]{:S(2)}) copy-start(f32[512,128]{1,0:T(8,128)} %param.10) | copy-start | bytes 786436
  11.9 26.5 %all-to-all-start = ((f32[32,1,512,4]{2,3,1,0:T(4,128)}), f32[32,1,512,4]{2,3,1,0:T(4,128)S(1)}, u32[]{:S(2)}, u32[]{:S(2)}) async-start(f32[32,1,512,4]{2,3,1,0:T(4,128)} %copy.153), calls=%async_computation | async-start | bytes 524288 | tf_op jit(solution)/shard_map/all_to_all | solution.py:11
  26.3 36.0 %copy-start.7 = (bf16[1,512,128]{1,0,2:T(2,128)(2,1)}, bf16[1,512,128]{1,0,2:T(2,128)(2,1)S(1)}, u32[]{:S(2)}) copy-start(bf16[1,512,128]{1,0,2:T(2,128)(2,1)S(1)} %copy.150) | copy-start | bytes 393220
  38.3 17.3 %all-to-all-start.2 = ((f32[1,512,128]{1,0,2:T(1,128)}), f32[1,512,128]{1,0,2:T(1,128)S(1)}, u32[]{:S(2)}, u32[]{:S(2)}) async-start(f32[1,512,128]{1,0,2:T(1,128)} %convert_multiply_fusion), calls=%async_computation.2 | async-start | bytes 524288 | tf_op jit(solution)/shard_map/all_to_all | solution.py:65
  55.6 18.1 %all-to-all-start.1 = ((f32[1,512,128]{1,0,2:T(1,128)}), f32[1,512,128]{1,0,2:T(1,128)S(1)}, u32[]{:S(2)}, u32[]{:S(2)}) async-start(f32[1,512,128]{1,0,2:T(1,128)} %copy.211), calls=%async_computation.1 | async-start | bytes 524288 | tf_op jit(solution)/shard_map/all_to_all | solution.py:66
  63.5 10.7 %copy-start.11 = (f32[16384]{0:T(1024)}, f32[16384]{0:T(1024)S(1)}, u32[]{:S(2)}) copy-start(f32[16384]{0:T(1024)S(1)} %fusion.52) | copy-start | bytes 196612
  65.0 9.9 %copy-start.1 = (f32[4,128,128]{1,2,0:T(8,128)}, f32[4,128,128]{1,2,0:T(8,128)S(1)}, u32[]{:S(2)}) copy-start(f32[4,128,128]{1,2,0:T(8,128)S(1)} %copy.165) | copy-start | bytes 786436
  74.1 0.7 copy-start.3
  79.4 2.9 copy-start.2
  79.4 2.8 copy-start.4
  109.6 3.2 copy-start
  121.9 1.9 copy-start.10
  135.3 1.0 copy-start.9
  135.3 1.0 copy-start.12
  135.3 1.0 copy-start.13
  234.3 182.0 %all-to-all-start.3 = ((f32[32,1,2048]{2,1,0:T(1,128)}), f32[32,1,2048]{2,1,0:T(1,128)S(1)}, u32[]{:S(2)}, u32[]{:S(2)}) async-start(f32[32,1,2048]{2,1,0:T(1,128)} %reshape.147), calls=%async_computation.3 | async-start | bytes 524288 | tf_op jit(solution)/shard_map/all_to_all | solution.py:103
  240.3 77.7 %all-reduce.3.cloned.1.call-start = ((), (), s32[]{:S(2)}) async-start(), calls=%async_computation.5 | async-start | bytes 524288 | tf_op jit(solution)/shard_map/psum | solution.py:101
  416.3 33.4 %all-to-all-start.4 = ((f32[32,1,2048]{2,1,0:T(1,128)}), f32[32,1,2048]{2,1,0:T(1,128)S(1)}, u32[]{:S(2)}, u32[]{:S(2)}) async-start(f32[32,1,2048]{2,1,0:T(1,128)} %reshape.149), calls=%async_computation.4 | async-start | bytes 524288 | tf_op jit(solution)/shard_map/all_to_all | solution.py:104
  442.8 5.6 %copy-start.6 = (f32[1,512,128]{1,0,2:T(1,128)S(1)}, f32[1,512,128]{1,0,2:T(1,128)}, u32[]{:S(2)}) copy-start(f32[1,512,128]{1,0,2:T(1,128)} %copy-done.5) | copy-start | bytes 786436
  442.8 5.6 %copy-start.8 = (bf16[1,512,128]{1,0,2:T(2,128)(2,1)S(1)}, bf16[1,512,128]{1,0,2:T(2,128)(2,1)}, u32[]{:S(2)}) copy-start(bf16[1,512,128]{1,0,2:T(2,128)(2,1)} %copy-done.7) | copy-start | bytes 393220
  442.8 5.6 %copy-start.17 = (f32[128]{0:T(128)S(1)}, f32[128]{0:T(128)}, u32[]{:S(2)}) copy-start(f32[128]{0:T(128)} %param.11) | copy-start | bytes 1540
Sparse Core Ops, SparseCore 0:
  244.3 73.6 all-reduce.2
